TPU v7x, 32 devices: a whole 2x2x4 slice. The times are simulated.
32 devices in a mesh: rep: 4 (over y, x), fsdp: 8 (over z, core).
Axes of the slice: x: 2, y: 2, z: 4, core: 2. Of those that a mesh axis runs over, the one named last changes fastest.
Arguments:
- pseudo_grad: float32 [4, 4096, 256], P('rep', 'fsdp'), may hold values from -6 to 6
- error_buf: float32 [4, 4096, 256], P('rep', 'fsdp'), may hold values from -6 to 6
- momentum: float32 [4096, 256], P('fsdp'), may hold values from -4 to 4
- params: float32 [4096, 256], P('fsdp'), may hold values from -6 to 6
- picks: int32 [4, 64], P('rep', 'fsdp'), may hold values from 0 to 511, as said below
Outputs:
- new_params: float32 [4096, 256], P('fsdp')
- new_momentum: float32 [4096, 256], P('fsdp')
- new_error: float32 [4, 4096, 256], P('rep', 'fsdp')
- gathered: bfloat16 [4096, 256], replicated
Inputs may be any that keep to these rules, and one draw needn't show every extreme that they name: `picks`: entries j of a row with the same j // 8 are distinct.
All inputs are finite; a program needn't handle non-finite values.
Results may differ from a plain program's by a relative error of at most 0.0017.
Values may be sent and summed in bfloat16 or wider, within the bound.
A program may use at most 64 MiB of HBM per device.

v0:
```python
import jax
import jax.numpy as jnp
from jax import lax
from jax.sharding import PartitionSpec as P

DECAY_RATE = 0.95
MOMENTUM_COEF = 0.9
STEP_SCALE = 0.7


def per_device(pseudo_grad, error_buf, momentum, params, picks):
    shard_blocks = params.shape[0]
    replicas = lax.axis_size("rep")
    accumulated = DECAY_RATE * error_buf[0] + pseudo_grad[0]
    own_picks = picks[0]
    positions = lax.iota(jnp.int32, shard_blocks)
    selector = (own_picks[:, None] == positions[None, :]).astype(jnp.float32)
    chosen_mask = jnp.sum(selector, axis=0)
    new_error = (accumulated * (1.0 - chosen_mask)[:, None])[None]
    chosen_values = jnp.dot(selector, accumulated, precision=lax.Precision.HIGHEST)
    all_values, all_picks = (
        lax.all_gather(chosen_values, "rep", axis=0, tiled=True),
        lax.all_gather(own_picks.astype(jnp.float32), "rep", axis=0, tiled=True),
    )
    spread = (all_picks[:, None] == positions.astype(jnp.float32)[None, :]).astype(jnp.float32)
    summed = lax.dot_general(
        spread, all_values, (((0,), (0,)), ((), ())), precision=lax.Precision.HIGHEST
    )
    delta = summed / replicas
    new_momentum = MOMENTUM_COEF * momentum + delta
    new_params = params - STEP_SCALE * (delta + MOMENTUM_COEF * new_momentum)
    gathered = lax.all_gather(new_params.astype(jnp.bfloat16), "fsdp", axis=0, tiled=True)
    return (new_params, new_momentum, new_error, gathered)


def solution(mesh):
    in_specs = (
        P("rep", "fsdp", None),
        P("rep", "fsdp", None),
        P("fsdp", None),
        P("fsdp", None),
        P("rep", "fsdp"),
    )
    out_specs = (P("fsdp", None), P("fsdp", None), P("rep", "fsdp", None), P())
    return jax.shard_map(
        per_device, mesh=mesh, in_specs=in_specs, out_specs=out_specs, check_vma=False
    )
```

profile of v0, /device:TPU:0, one launch (start us, length us, event | category | flops | bytes accessed | tf_op | source)
XLA Modules:
  0.0 72.3 jit_solution(16122513474063554046)
XLA Ops:
  7.2 0.0 copy-start.2
  7.2 0.0 copy-start
  7.2 0.0 copy-start.1
  7.2 0.0 all-gather.2.cloned.1.call-start
  7.3 1.6 %fusion = f32[8,256]{1,0:T(8,128)S(1)} fusion(f32[1,512,256]{2,1,0:T(8,128)} %param.5, f32[1,512,256]{2,1,0:T(8,128)} %param.6, s32[8]{0:T(128)} %bitcast.7), kind=kOutput, calls=%fused_computation.1 | convolution fusion | flops 12849152 | bytes 1056800 | tf_op jit(solution)/shard_map/dot_general | solution.py:20
  8.8 9.6 %all_gather.10 = f32[32,256]{1,0:T(8,128)S(1)} all-gather(f32[8,256]{1,0:T(8,128)S(1)} %fusion), channel_id=1, replica_groups=mesh['rep'=4,'fsdp'=8] {'rep'}, dimensions={0}, use_global_device_ids=true | all-gather | bytes 40960 | tf_op jit(solution)/shard_map/all_gather | solution.py:22
  18.5 1.2 %dynamic-slice = u32[1]{0:T(128)} dynamic-slice(u32[32]{0:T(128)} %constant.18, u32[]{:T(128)S(6)} %add.17), dynamic_slice_sizes={1} | dynamic-slice | bytes 12
  20.4 0.8 %convert_dynamic-update-slice_fusion = f32[32]{0:T(128)S(1)} fusion(f32[32]{0:T(128)S(1)} %broadcast.16, u32[]{:T(128)} %bitcast.1, s32[1,8]{1,0:T(1,128)} %param.9), kind=kLoop, calls=%fused_computation.15 | loop fusion | flops 8 | bytes 164
  21.1 8.9 %all-reduce = f32[32]{0:T(128)S(1)} all-reduce(f32[32]{0:T(128)S(1)} %convert_dynamic-update-slice_fusion), channel_id=1, replica_groups=mesh['rep'=4,'fsdp'=8] {'rep'}, use_global_device_ids=true, to_apply=%add | all-reduce | flops 32 | bytes 256
  30.1 2.8 %fusion.7 = (bf16[512,256]{1,0:T(8,128)(2,1)}, f32[512,256]{1,0:T(8,128)}, f32[512,256]{1,0:T(8,128)}) fusion(f32[512,256]{1,0:T(8,128)} %param.8, f32[512,256]{1,0:T(8,128)} %param.7, f32[32,256]{1,0:T(8,128)S(1)} %all_gather.10, f32[512]{0:T(512)S(1)} %iota_convert_fusion, f32[32]{0:T(128)S(1)} %all-reduce), kind=kOutput, calls=%fused_computation.17 | convolution fusion | flops 51396608 | bytes 2394240 | tf_op jit(solution)/shard_map/dot_general | solution.py:26
  32.9 0.0 all-gather.2.cloned.1.call-update
  32.9 0.0 copy-done.2
  32.9 0.1 convert_reduce_fusion
  33.0 0.0 copy-done
  33.0 0.0 copy-done.1
  33.0 0.9 %broadcast_multiply_fusion = f32[1,512,256]{2,1,0:T(8,128)} fusion(f32[512]{0:T(512)S(1)} %broadcast_subtract_fusion, f32[1,512,256]{2,1,0:T(8,128)S(1)} %copy-done, f32[1,512,256]{2,1,0:T(8,128)S(1)} %copy-done.1), kind=kLoop, calls=%fused_computation.6 | loop fusion | flops 393216 | bytes 1574912 | tf_op jit(solution)/shard_map/mul | solution.py:19
  33.9 28.5 %all-gather.2.cloned.1.call-done = bf16[4096,256]{1,0:T(8,128)(2,1)} async-done(((bf16[512,256]{1,0:T(8,128)(2,1)}), bf16[4096,256]{1,0:T(8,128)(2,1)}) %all-gather.2.cloned.1.call-update) | async-done | bytes 2097168 | tf_op jit(solution)/shard_map/all_gather | solution.py:32
  62.4 3.0 %copy.11 = bf16[4096,256]{1,0:T(8,128)(2,1)} copy(bf16[4096,256]{1,0:T(8,128)(2,1)} %all-gather.2.cloned.1.call-done) | data formatting | bytes 4194304
  (3 shorter events, 0.0 us)
Async XLA Ops:
  7.2 25.7 %copy-start.2 = (s32[1,8]{1,0:T(1,128)S(1)}, s32[1,8]{1,0:T(1,128)}, u32[]{:S(2)}) copy-start(s32[1,8]{1,0:T(1,128)} %param.9) | copy-start | bytes 100
  7.2 25.8 %copy-start = (f32[1,512,256]{2,1,0:T(8,128)S(1)}, f32[1,512,256]{2,1,0:T(8,128)}, u32[]{:S(2)}) copy-start(f32[1,512,256]{2,1,0:T(8,128)} %param.5) | copy-start | bytes 1572868
  7.2 25.8 %copy-start.1 = (f32[1,512,256]{2,1,0:T(8,128)S(1)}, f32[1,512,256]{2,1,0:T(8,128)}, u32[]{:S(2)}) copy-start(f32[1,512,256]{2,1,0:T(8,128)} %param.6) | copy-start | bytes 1572868
  7.2 55.2 %all-gather.2.cloned.1.call-start = ((), (), s32[]{:S(2)}) async-start(), calls=%async_computation | async-start | bytes 2359296 | tf_op jit(solution)/shard_map/all_gather | solution.py:32
Sparse Core Ops, SparseCore 0:
  33.0 29.3 all-gather.1
where the time goes:
time: 72.6 us; the launch traced here: 72.3 us
  waiting for transfers between devices  28.5 us (39%)
  blocking collectives  18.6 us (26%)
  between operations  14.7 us (20%)
  matrix products  4.36 us (6%)
  local copies, waits for them, and re-layouts  4.3 us (6%)
  other arithmetic  1.78 us (2%)
    all_gather x1, waiting for transfers between devices, per_device(): lax.all_gather(new_params.astype(jnp.bfloat16), 'fsdp', axis=0, tiled=True)  28.5 us
    all_gather x1, blocking collectives, per_device(): lax.all_gather(chosen_values, 'rep', axis=0, tiled=True)  9.65 us
    unnamed x1, blocking collectives  8.92 us
    unnamed x9, local copies, waits for them, and re-layouts  4.3 us
    dot_general x1, matrix products, per_device(): lax.dot_general(spread, all_values, (((0,), (0,)), ((), ())), precision=l...  2.8 us
    dot_general x1, matrix products, per_device(): jnp.dot(selector, accumulated, precision=lax.Precision.HIGHEST)  1.57 us
  transfers between devices with their start and end apart: 1, of which 1 were waited for; matrix products, arithmetic and copies ran while one was open for 1% of the time, Pallas kernels for 0%

commit v1 on v0

v1 whole, which is shorter than its diff:
```python
import functools

import jax
import jax.numpy as jnp
from jax import lax
from jax.experimental import pallas as pl
from jax.experimental.pallas import tpu as pltpu
from jax.sharding import PartitionSpec as P

DECAY_RATE = 0.95
MOMENTUM_COEF = 0.9
STEP_SCALE = 0.7
MESH = pl.DeviceIdType.MESH


def exchange_kernel(
    replicas, shards, topk, picks_hbm, grad_hbm, error_hbm, momentum_hbm, params_hbm,
    params_out, momentum_out, error_out, gathered,
    picks_ref, grad, error, momentum, params, payload,
    in_sem, pay_send, pay_recv, z_send, z_recv, plane_send, plane_recv, core_send, core_recv,
):
    rep, fsdp = lax.axis_index("rep"), lax.axis_index("fsdp")
    groups = shards // 2
    group, core = fsdp // 2, fsdp % 2
    rows, width = grad.shape
    part = rows // replicas

    def mate(offset):
        return (lax.rem(rep + offset, replicas), fsdp)

    def along(offset):
        return (rep, lax.rem(group + offset, groups) * 2 + core)

    sibling = (rep, group * 2 + 1 - core)

    def remote(src, dst, send, recv, device):
        return pltpu.make_async_remote_copy(
            src_ref=src, dst_ref=dst, send_sem=send, recv_sem=recv, device_id=device, device_id_type=MESH
        )

    barrier = pltpu.get_barrier_semaphore()
    partners = [mate(m) for m in range(1, replicas)] + [along(d) for d in range(1, groups)] + [sibling]
    for device in partners:
        pl.semaphore_signal(barrier, inc=1, device_id=device, device_id_type=MESH)

    loads = [
        pltpu.make_async_copy(src, dst, in_sem.at[i])
        for i, (src, dst) in enumerate(
            ((grad_hbm.at[0], grad), (error_hbm.at[0], error), (momentum_hbm, momentum),
             (params_hbm, params), (picks_hbm, picks_ref))
        )
    ]
    loads[4].start()
    for load in loads[:4]:
        load.start()
    loads[4].wait()
    loads[0].wait()
    loads[1].wait()

    for j in range(topk):
        pick = picks_ref[0, j]
        payload[0, j, :] = DECAY_RATE * error[pick, :] + grad[pick, :]
        payload[0, topk + j, :] = jnp.full((width,), pick.astype(jnp.float32))
    pl.semaphore_wait(barrier, len(partners))
    pays = [
        remote(payload.at[0], payload.at[m], pay_send.at[m], pay_recv.at[m], mate(m)) for m in range(1, replicas)
    ]
    for pay in pays:
        pay.start()

    positions = lax.broadcasted_iota(jnp.int32, (rows, width), 0)
    hit = positions == picks_ref[0, 0]
    for j in range(1, topk):
        hit = jnp.logical_or(hit, positions == picks_ref[0, j])
    error_out[...] = jnp.where(hit, 0.0, DECAY_RATE * error[...] + grad[...])
    loads[2].wait()
    loads[3].wait()

    lanes = lax.broadcasted_iota(jnp.int32, (topk, rows), 1).astype(jnp.float32)
    for pay in pays:
        pay.wait_recv()
    spread = jnp.concatenate(
        [(payload[m, topk : 2 * topk, 0:1] == lanes).astype(jnp.float32) for m in range(replicas)], axis=0
    )
    values = jnp.concatenate([payload[m, :topk, :] for m in range(replicas)], axis=0)
    summed = lax.dot_general(
        spread, values, (((0,), (0,)), ((), ())),
        precision=lax.Precision.HIGHEST, preferred_element_type=jnp.float32,
    )
    delta = summed / replicas
    new_momentum = MOMENTUM_COEF * momentum[...] + delta
    new_params = params[...] - STEP_SCALE * (delta + MOMENTUM_COEF * new_momentum)
    own_rows = pl.ds(pl.multiple_of(fsdp * rows, rows), rows)
    gathered[own_rows, :] = new_params.astype(jnp.bfloat16)

    def piece(g, c, s):
        return gathered.at[pl.ds(pl.multiple_of((g * 2 + c) * rows + s * part, part), part), :]

    sends = []

    def go(copy):
        copy.start()
        sends.append(copy)
        return copy

    outs = []
    for d in range(1, groups):
        own = piece(group, core, rep)
        outs.append(go(remote(own, own, z_send.at[d], z_recv.at[d], along(d))))
    whole = gathered.at[own_rows, :]
    siblings = [go(remote(whole, whole, core_send.at[0, 0], core_recv.at[0, 0], sibling))]
    params_out[...] = new_params
    momentum_out[...] = new_momentum

    planes = {}
    for d in range(1, groups):
        outs[d - 1].wait_recv()
        source = lax.rem(group + groups - d, groups)
        got = piece(source, core, rep)
        for m in range(1, replicas):
            planes[d, m] = go(remote(got, got, plane_send.at[d, m], plane_recv.at[d, m], mate(m)))
        siblings.append(go(remote(got, got, core_send.at[d, 0], core_recv.at[d, 0], sibling)))
    for d in range(1, groups):
        source = lax.rem(group + groups - d, groups)
        for m in range(1, replicas):
            planes[d, m].wait_recv()
            got = piece(source, core, lax.rem(rep + replicas - m, replicas))
            siblings.append(go(remote(got, got, core_send.at[d, m], core_recv.at[d, m], sibling)))
    for copy in siblings:
        copy.wait_recv()
    for pay in pays:
        pay.wait_send()
    for copy in sends:
        copy.wait_send()


def write_kernel(params, momentum, error, gathered, params_out, momentum_out, error_out, gathered_out, sem):
    pairs = ((gathered, gathered_out), (params, params_out), (momentum, momentum_out), (error, error_out.at[0]))
    copies = [pltpu.make_async_copy(src, dst, sem.at[i]) for i, (src, dst) in enumerate(pairs)]
    for copy in copies:
        copy.start()
    for copy in copies:
        copy.wait()


def per_device(replicas, shards, pseudo_grad, error_buf, momentum, params, picks):
    rows, width = params.shape
    topk = picks.shape[1]
    groups = shards // 2
    f32, bf16 = jnp.float32, jnp.bfloat16
    shard = (rows, width)
    dma = pltpu.SemaphoreType.DMA
    vmem = pl.BlockSpec(memory_space=pltpu.VMEM)
    hbm = pl.BlockSpec(memory_space=pltpu.HBM)
    held = pl.pallas_call(
        functools.partial(exchange_kernel, replicas, shards, topk),
        out_shape=(
            pltpu.VMEM(shard, f32),
            pltpu.VMEM(shard, f32),
            pltpu.VMEM(shard, f32),
            pltpu.VMEM((shards * rows, width), bf16),
        ),
        in_specs=[hbm] * 5,
        out_specs=[vmem] * 4,
        scratch_shapes=[
            pltpu.SMEM((1, topk), jnp.int32),
            pltpu.VMEM(shard, f32),
            pltpu.VMEM(shard, f32),
            pltpu.VMEM(shard, f32),
            pltpu.VMEM(shard, f32),
            pltpu.VMEM((replicas, 2 * topk, width), f32),
            dma((5,)),
            dma((replicas,)),
            dma((replicas,)),
            dma((groups,)),
            dma((groups,)),
            dma((groups, replicas)),
            dma((groups, replicas)),
            dma((groups, replicas)),
            dma((groups, replicas)),
        ],
        compiler_params=pltpu.CompilerParams(
            collective_id=0, has_side_effects=True, vmem_limit_bytes=32 * 1024 * 1024
        ),
        name="exchange",
    )(*(pltpu.with_memory_space_constraint(x, pltpu.HBM) for x in (picks, pseudo_grad, error_buf, momentum, params)))
    return pl.pallas_call(
        write_kernel,
        out_shape=(
            jax.ShapeDtypeStruct(shard, f32),
            jax.ShapeDtypeStruct(shard, f32),
            jax.ShapeDtypeStruct((1, rows, width), f32),
            jax.ShapeDtypeStruct((shards * rows, width), bf16),
        ),
        in_specs=[vmem] * 4,
        out_specs=[hbm] * 4,
        scratch_shapes=[dma((4,))],
        name="write_out",
    )(*held)


def solution(mesh):
    in_specs = (
        P("rep", "fsdp", None),
        P("rep", "fsdp", None),
        P("fsdp", None),
        P("fsdp", None),
        P("rep", "fsdp"),
    )
    out_specs = (P("fsdp", None), P("fsdp", None), P("rep", "fsdp", None), P())
    step = functools.partial(per_device, mesh.shape["rep"], mesh.shape["fsdp"])
    return jax.shard_map(step, mesh=mesh, in_specs=in_specs, out_specs=out_specs, check_vma=False)
```

time: 72.6 us -> 32.2 us (0.44)
  waiting for transfers between devices: 28.5 us -> 0 us
  Pallas kernels: 0 us -> 27.7 us
  blocking collectives: 18.6 us -> 0 us
  between operations: 14.7 us -> 0.65 us
  matrix products: 4.36 us -> 0 us
  other arithmetic: 1.78 us -> 0 us
    all_gather x1 -> x0, waiting for transfers between devices: 28.5 us -> none  [per_device(): lax.all_gather(new_params.astype(jnp.bfloat16), 'fsdp', axis=0, tiled=True)]
    pallas_call x0 -> x2, Pallas kernels: none -> 27.7 us  [the longest x1 23.7 us: per_device(): pl.pallas_call(functools.partial(exchange_kernel, replicas, shards, topk)...]
    all_gather x1 -> x0, blocking collectives: 9.65 us -> none  [per_device(): lax.all_gather(chosen_values, 'rep', axis=0, tiled=True)]
    unnamed x1 -> x0, blocking collectives: 8.92 us -> none
    dot_general x2 -> x0, matrix products: 4.36 us -> none  [the longest x1 2.8 us: per_device(): lax.dot_general(spread, all_values, (((0,), (0,)), ((), ())), precision=l...]
    mul x1 -> x0, other arithmetic: 0.93 us -> none  [per_device(): new_error = (accumulated * (1.0 - chosen_mask)[:, None])[None]]
    unnamed x1 -> x0, other arithmetic: 0.75 us -> none
    unnamed x9 -> x8, local copies, waits for them, and re-layouts: 4.3 us -> 3.7 us
  transfers between devices with their start and end apart: 1 -> 0, of which waited for: 1 -> 0; matrix products, arithmetic and copies ran while one was open for 1% -> 0% of each run, Pallas kernels for 0% -> 0%
where the time goes in v1:
time: 32.2 us; the launch traced here: 32 us
  Pallas kernels  27.7 us (86%)
  local copies, waits for them, and re-layouts  3.7 us (11%)
  between operations  0.65 us (2%)
    pallas_call x1, Pallas kernels, per_device(): pl.pallas_call(functools.partial(exchange_kernel, replicas, shards, topk)...  23.7 us
    pallas_call x1, Pallas kernels, per_device(): pl.pallas_call(write_kernel, out_shape=(jax.ShapeDtypeStruct(shard, f32),...  3.94 us
    unnamed x8, local copies, waits for them, and re-layouts  3.7 us

profile of v1, /device:TPU:0, one launch (start us, length us, event | category | flops | bytes accessed | tf_op | source)
XLA Modules:
  0.0 32.0 jit_solution(13878772231833147105)
XLA Ops:
  0.6 23.7 %exchange.1 = (f32[512,256]{1,0:T(8,128)S(1)}, f32[512,256]{1,0:T(8,128)S(1)}, f32[512,256]{1,0:T(8,128)S(1)}, bf16[4096,256]{1,0:T(8,128)(2,1)S(1)}) custom-call(s32[1,8]{1,0:T(1,128)} %picks_hbm.1, f32[1,512,256]{2,1,0:T(8,128)} %grad_hbm.1, f32[1,512,256]{2,1,0:T(8,128)} %error_hbm.1, f32[512,256]{1,0:T(8,128)} %momentum_hbm.1, f32[512,256]{1,0:T(8,128)} %params_hbm.1), custom_call_target="tpu_custom_call" | custom-call | tf_op jit(solution)/shard_map/exchange/pallas_call | solution.py:155
  24.4 0.0 copy-start
  24.4 1.3 %copy-done = bf16[4096,256]{1,0:T(8,128)(2,1)} copy-done((bf16[4096,256]{1,0:T(8,128)(2,1)}, bf16[4096,256]{1,0:T(8,128)(2,1)S(1)}, u32[]{:S(2)}) %copy-start) | copy-done | bytes 2097176
  25.7 0.0 copy-start.1
  25.7 0.8 %copy-done.1 = f32[512,256]{1,0:T(8,128)} copy-done((f32[512,256]{1,0:T(8,128)}, f32[512,256]{1,0:T(8,128)S(1)}, u32[]{:S(2)}) %copy-start.1) | copy-done | bytes 524312
  26.5 0.0 copy-start.2
  26.5 0.8 %copy-done.2 = f32[512,256]{1,0:T(8,128)} copy-done((f32[512,256]{1,0:T(8,128)}, f32[512,256]{1,0:T(8,128)S(1)}, u32[]{:S(2)}) %copy-start.2) | copy-done | bytes 524312
  27.3 0.0 copy-start.3
  27.3 0.8 %copy-done.3 = f32[512,256]{1,0:T(8,128)} copy-done((f32[512,256]{1,0:T(8,128)}, f32[512,256]{1,0:T(8,128)S(1)}, u32[]{:S(2)}) %copy-start.3) | copy-done | bytes 524312
  28.1 3.9 %write_out.1 = (f32[512,256]{1,0:T(8,128)}, f32[512,256]{1,0:T(8,128)}, f32[1,512,256]{2,1,0:T(8,128)}, bf16[4096,256]{1,0:T(8,128)(2,1)}) custom-call(f32[512,256]{1,0:T(8,128)} %copy-done.1, f32[512,256]{1,0:T(8,128)} %copy-done.2, f32[512,256]{1,0:T(8,128)} %copy-done.3, bf16[4096,256]{1,0:T(8,128)(2,1)} %copy-done), custom_call_target="tpu_custom_call" | custom-call | tf_op jit(solution)/shard_map/write_out/pallas_call | solution.py:187
Async XLA Ops:
  24.4 1.3 %copy-start = (bf16[4096,256]{1,0:T(8,128)(2,1)}, bf16[4096,256]{1,0:T(8,128)(2,1)S(1)}, u32[]{:S(2)}) copy-start(bf16[4096,256]{1,0:T(8,128)(2,1)S(1)} %get-tuple-element.11.gathered) | copy-start | bytes 6291460
  25.7 0.8 %copy-start.1 = (f32[512,256]{1,0:T(8,128)}, f32[512,256]{1,0:T(8,128)S(1)}, u32[]{:S(2)}) copy-start(f32[512,256]{1,0:T(8,128)S(1)} %get-tuple-element.8.params) | copy-start | bytes 1572868
  26.5 0.8 %copy-start.2 = (f32[512,256]{1,0:T(8,128)}, f32[512,256]{1,0:T(8,128)S(1)}, u32[]{:S(2)}) copy-start(f32[512,256]{1,0:T(8,128)S(1)} %get-tuple-element.9.momentum) | copy-start | bytes 1572868
  27.3 0.8 %copy-start.3 = (f32[512,256]{1,0:T(8,128)}, f32[512,256]{1,0:T(8,128)S(1)}, u32[]{:S(2)}) copy-start(f32[512,256]{1,0:T(8,128)S(1)} %get-tuple-element.10.error) | copy-start | bytes 1572868

commit v2 on v1

--- a/solution.py
+++ b/solution.py
@@ -57,14 +57,16 @@
     loads[0].wait()
     loads[1].wait()
 
+    lane = lax.broadcasted_iota(jnp.int32, (1, width), 1)
+    numbers = jnp.zeros((1, width), jnp.float32)
     for j in range(topk):
         pick = picks_ref[0, j]
-        payload[0, j, :] = DECAY_RATE * error[pick, :] + grad[pick, :]
-        payload[0, topk + j, :] = jnp.full((width,), pick.astype(jnp.float32))
+        payload[rep, j, :] = DECAY_RATE * error[pick, :] + grad[pick, :]
+        numbers = jnp.where(lane == rep * topk + j, (pick + 1).astype(jnp.float32), numbers)
+    payload[rep, topk : 2 * topk, :] = jnp.broadcast_to(numbers, (topk, width))
     pl.semaphore_wait(barrier, len(partners))
-    pays = [
-        remote(payload.at[0], payload.at[m], pay_send.at[m], pay_recv.at[m], mate(m)) for m in range(1, replicas)
-    ]
+    own_pay = payload.at[rep]
+    pays = [remote(own_pay, own_pay, pay_send.at[m], pay_recv.at[m], mate(m)) for m in range(1, replicas)]
     for pay in pays:
         pay.start()
 
@@ -76,56 +78,100 @@
     loads[2].wait()
     loads[3].wait()
 
-    lanes = lax.broadcasted_iota(jnp.int32, (topk, rows), 1).astype(jnp.float32)
     for pay in pays:
         pay.wait_recv()
-    spread = jnp.concatenate(
-        [(payload[m, topk : 2 * topk, 0:1] == lanes).astype(jnp.float32) for m in range(replicas)], axis=0
-    )
+    named = sum(payload[m, topk : topk + 1, :] for m in range(replicas))
     values = jnp.concatenate([payload[m, :topk, :] for m in range(replicas)], axis=0)
-    summed = lax.dot_general(
-        spread, values, (((0,), (0,)), ((), ())),
-        precision=lax.Precision.HIGHEST, preferred_element_type=jnp.float32,
-    )
-    delta = summed / replicas
-    new_momentum = MOMENTUM_COEF * momentum[...] + delta
-    new_params = params[...] - STEP_SCALE * (delta + MOMENTUM_COEF * new_momentum)
-    own_rows = pl.ds(pl.multiple_of(fsdp * rows, rows), rows)
-    gathered[own_rows, :] = new_params.astype(jnp.bfloat16)
-
-    def piece(g, c, s):
-        return gathered.at[pl.ds(pl.multiple_of((g * 2 + c) * rows + s * part, part), part), :]
-
-    sends = []
+    parts, rest = [], values
+    for _ in range(3):
+        parts.append(rest.astype(jnp.bfloat16))
+        rest = rest - parts[-1].astype(jnp.float32)
+    places = (lax.broadcasted_iota(jnp.int32, (part, width), 0) + 1).astype(jnp.float32)
+
+    def update(s):
+        here = pl.ds(pl.multiple_of(s * part, part), part)
+        spread = (places + (s * part).astype(jnp.float32) == named).astype(jnp.float32)
+        spread = spread[:, : replicas * topk].astype(jnp.bfloat16)
+        summed = sum(jnp.dot(spread, piece, preferred_element_type=jnp.float32) for piece in reversed(parts))
+        delta = summed / replicas
+        new_momentum = MOMENTUM_COEF * momentum[here, :] + delta
+        new_params = params[here, :] - STEP_SCALE * (delta + MOMENTUM_COEF * new_momentum)
+        gathered[pl.ds(pl.multiple_of(fsdp * rows + s * part, part), part), :] = new_params.astype(jnp.bfloat16)
+        params_out[here, :] = new_params
+        momentum_out[here, :] = new_momentum
+
+    def piece(g, s, start=0, count=part):
+        first = (g * 2 + core) * rows + s * part + start
+        return gathered.at[pl.ds(pl.multiple_of(first, count), count), :]
+
+    sends, siblings = [], []
 
     def go(copy):
         copy.start()
         sends.append(copy)
         return copy
 
-    outs = []
-    for d in range(1, groups):
-        own = piece(group, core, rep)
-        outs.append(go(remote(own, own, z_send.at[d], z_recv.at[d], along(d))))
-    whole = gathered.at[own_rows, :]
-    siblings = [go(remote(whole, whole, core_send.at[0, 0], core_recv.at[0, 0], sibling))]
-    params_out[...] = new_params
-    momentum_out[...] = new_momentum
-
-    planes = {}
-    for d in range(1, groups):
+    def share(ref, at):
+        siblings.append(go(remote(ref, ref, core_send.at[at], core_recv.at[at], sibling)))
+
+    update(rep)
+    own = piece(group, rep)
+    outs = [go(remote(own, own, z_send.at[d], z_recv.at[d], along(d))) for d in range(1, groups)]
+    for m in range(1, replicas):
+        update(lax.rem(rep + m, replicas))
+    whole = gathered.at[pl.ds(pl.multiple_of(fsdp * rows, rows), rows), :]
+    share(whole, (0, 0))
+
+    x, y = rep % 2, rep // 2
+    lines = replicas // 2
+    half = part // 2
+    across = (y * 2 + 1 - x, fsdp)
+
+    def line(offset):
+        return lax.rem(y + offset, lines)
+
+    def source(d):
+        return lax.rem(group + groups - d, groups)
+
+    def z_stage(d):
         outs[d - 1].wait_recv()
-        source = lax.rem(group + groups - d, groups)
-        got = piece(source, core, rep)
-        for m in range(1, replicas):
-            planes[d, m] = go(remote(got, got, plane_send.at[d, m], plane_recv.at[d, m], mate(m)))
-        siblings.append(go(remote(got, got, core_send.at[d, 0], core_recv.at[d, 0], sibling)))
-    for d in range(1, groups):
-        source = lax.rem(group + groups - d, groups)
-        for m in range(1, replicas):
-            planes[d, m].wait_recv()
-            got = piece(source, core, lax.rem(rep + replicas - m, replicas))
-            siblings.append(go(remote(got, got, core_send.at[d, m], core_recv.at[d, m], sibling)))
+        got = piece(source(d), rep)
+        copies[d] = [go(remote(got, got, plane_send.at[d, 0], plane_recv.at[d, 0], across))]
+        for m in range(1, lines):
+            to = (line(m) * 2 + x, fsdp)
+            copies[d].append(go(remote(got, got, plane_send.at[d, m], plane_recv.at[d, m], to)))
+        share(got, (d, 0))
+
+    def plane_stage(d):
+        firsts[d], seconds[d] = [], []
+        copies[d][0].wait_recv()
+        got = piece(source(d), y * 2 + 1 - x)
+        first = piece(source(d), y * 2 + 1 - x, 0, half)
+        for m in range(1, lines):
+            at = lines + m
+            to = (line(m) * 2 + x, fsdp)
+            firsts[d].append(go(remote(first, first, plane_send.at[d, at], plane_recv.at[d, at], to)))
+        share(got, (d, 1))
+        for m in range(1, lines):
+            copies[d][m].wait_recv()
+            s = line(lines - m) * 2 + x
+            second = piece(source(d), s, half, half)
+            at = 2 * lines + m
+            seconds[d].append(go(remote(second, second, plane_send.at[d, at], plane_recv.at[d, at], across)))
+            share(piece(source(d), s), (d, 1 + m))
+
+    def last_stage(d):
+        for m in range(1, lines):
+            s = line(lines - m) * 2 + 1 - x
+            firsts[d][m - 1].wait_recv()
+            seconds[d][m - 1].wait_recv()
+            share(piece(source(d), s), (d, lines + m))
+
+    copies, firsts, seconds = {}, {}, {}
+    for turn in range(1, groups + 2):
+        for stage, late in ((z_stage, 0), (plane_stage, 1), (last_stage, 2)):
+            if 1 <= turn - late < groups:
+                stage(turn - late)
     for copy in siblings:
         copy.wait_recv()
     for pay in pays:
@@ -174,8 +220,8 @@
             dma((replicas,)),
             dma((groups,)),
             dma((groups,)),
-            dma((groups, replicas)),
-            dma((groups, replicas)),
+            dma((groups, 3 * replicas // 2)),
+            dma((groups, 3 * replicas // 2)),
             dma((groups, replicas)),
             dma((groups, replicas)),
         ],
@@ -195,8 +241,9 @@
         in_specs=[vmem] * 4,
         out_specs=[hbm] * 4,
         scratch_shapes=[dma((4,))],
+        compiler_params=pltpu.CompilerParams(vmem_limit_bytes=16 * 1024 * 1024),
         name="write_out",
-    )(*held)
+    )(*(pltpu.with_memory_space_constraint(x, pltpu.VMEM) for x in held))
 
 
 def solution(mesh):

time: 32.2 us -> 28.6 us (0.89)
  local copies, waits for them, and re-layouts: 3.7 us -> 0 us
    unnamed x8 -> x0, local copies, waits for them, and re-layouts: 3.7 us -> none
    pallas_call x1, Pallas kernels: 23.7 us -> 25.9 us  [per_device(): pl.pallas_call(functools.partial(exchange_kernel, replicas, shards, topk)...]
    pallas_call x1, Pallas kernels: 3.94 us -> 1.86 us  [per_device(): pl.pallas_call(write_kernel, out_shape=(jax.ShapeDtypeStruct(shard, f32),...]
where the time goes in v2:
time: 28.6 us; the launch traced here: 28.4 us
  Pallas kernels  27.8 us (97%)
  between operations  0.64 us (2%)
    pallas_call x1, Pallas kernels, per_device(): pl.pallas_call(functools.partial(exchange_kernel, replicas, shards, topk)...  25.9 us
    pallas_call x1, Pallas kernels, per_device(): pl.pallas_call(write_kernel, out_shape=(jax.ShapeDtypeStruct(shard, f32),...  1.86 us

profile of v2, /device:TPU:0, one launch (start us, length us, event | category | flops | bytes accessed | tf_op | source)
XLA Modules:
  0.0 28.4 jit_solution(14563527374796622606)
XLA Ops:
  0.6 25.9 %exchange.1 = (f32[512,256]{1,0:T(8,128)S(1)}, f32[512,256]{1,0:T(8,128)S(1)}, f32[512,256]{1,0:T(8,128)S(1)}, bf16[4096,256]{1,0:T(8,128)(2,1)S(1)}) custom-call(s32[1,8]{1,0:T(1,128)} %picks_hbm.1, f32[1,512,256]{2,1,0:T(8,128)} %grad_hbm.1, f32[1,512,256]{2,1,0:T(8,128)} %error_hbm.1, f32[512,256]{1,0:T(8,128)} %momentum_hbm.1, f32[512,256]{1,0:T(8,128)} %params_hbm.1), custom_call_target="tpu_custom_call" | custom-call | tf_op jit(solution)/shard_map/exchange/pallas_call | solution.py:201
  26.5 1.9 %write_out.1 = (f32[512,256]{1,0:T(8,128)}, f32[512,256]{1,0:T(8,128)}, f32[1,512,256]{2,1,0:T(8,128)}, bf16[4096,256]{1,0:T(8,128)(2,1)}) custom-call(f32[512,256]{1,0:T(8,128)S(1)} %get-tuple-element.8.params, f32[512,256]{1,0:T(8,128)S(1)} %get-tuple-element.9.momentum, f32[512,256]{1,0:T(8,128)S(1)} %get-tuple-element.10.error, ...), custom_call_target="tpu_custom_call" | custom-call | tf_op jit(solution)/shard_map/write_out/pallas_call | solution.py:233

commit v3 on v1

--- a/solution.py
+++ b/solution.py
@@ -15,15 +15,18 @@
 
 def exchange_kernel(
     replicas, shards, topk, picks_hbm, grad_hbm, error_hbm, momentum_hbm, params_hbm,
-    params_out, momentum_out, error_out, gathered,
-    picks_ref, grad, error, momentum, params, payload,
+    params_out, momentum_out, error_out, final,
+    picks_ref, grad, error, momentum, params, payload, gathered, fixes,
     in_sem, pay_send, pay_recv, z_send, z_recv, plane_send, plane_recv, core_send, core_recv,
+    fix_send, fix_recv, fix_core_send, fix_core_recv,
 ):
     rep, fsdp = lax.axis_index("rep"), lax.axis_index("fsdp")
     groups = shards // 2
     group, core = fsdp // 2, fsdp % 2
     rows, width = grad.shape
     part = rows // replicas
+    named_rows = replicas * topk
+    f32, bf16 = jnp.float32, jnp.bfloat16
 
     def mate(offset):
         return (lax.rem(rep + offset, replicas), fsdp)
@@ -46,90 +49,128 @@
     loads = [
         pltpu.make_async_copy(src, dst, in_sem.at[i])
         for i, (src, dst) in enumerate(
-            ((grad_hbm.at[0], grad), (error_hbm.at[0], error), (momentum_hbm, momentum),
-             (params_hbm, params), (picks_hbm, picks_ref))
+            ((picks_hbm, picks_ref), (momentum_hbm, momentum), (params_hbm, params),
+             (grad_hbm.at[0], grad), (error_hbm.at[0], error))
         )
     ]
-    loads[4].start()
-    for load in loads[:4]:
+    for load in loads:
         load.start()
+    for load in loads[:3]:
+        load.wait()
+
+    def step(moment, weight, delta):
+        new_momentum = MOMENTUM_COEF * moment + delta
+        return new_momentum, weight - STEP_SCALE * (delta + MOMENTUM_COEF * new_momentum)
+
+    own_rows = pl.ds(pl.multiple_of(fsdp * rows, rows), rows)
+    gathered[own_rows, :] = step(momentum[...], params[...], 0.0)[1].astype(bf16)
+
+    loads[3].wait()
     loads[4].wait()
-    loads[0].wait()
-    loads[1].wait()
-
+    lane = lax.broadcasted_iota(jnp.int32, (1, width), 1)
+    numbers = jnp.zeros((1, width), f32)
     for j in range(topk):
         pick = picks_ref[0, j]
-        payload[0, j, :] = DECAY_RATE * error[pick, :] + grad[pick, :]
-        payload[0, topk + j, :] = jnp.full((width,), pick.astype(jnp.float32))
+        payload[rep, j, :] = DECAY_RATE * error[pick, :] + grad[pick, :]
+        numbers = jnp.where(lane == rep * topk + j, (pick + 1).astype(f32), numbers)
+    payload[rep, topk : 2 * topk, :] = jnp.broadcast_to(numbers, (topk, width))
     pl.semaphore_wait(barrier, len(partners))
-    pays = [
-        remote(payload.at[0], payload.at[m], pay_send.at[m], pay_recv.at[m], mate(m)) for m in range(1, replicas)
-    ]
-    for pay in pays:
-        pay.start()
+
+    def piece(g, s):
+        return gathered.at[pl.ds(pl.multiple_of((g * 2 + core) * rows + s * part, part), part), :]
+
+    def source(d):
+        return lax.rem(group + groups - d, groups)
+
+    sends, siblings, planes = [], {}, {}
+
+    def go(copy):
+        copy.start()
+        sends.append(copy)
+        return copy
+
+    def share(ref, d, m):
+        siblings[d, m] = go(remote(ref, ref, core_send.at[d, m], core_recv.at[d, m], sibling))
+
+    own_pay = payload.at[rep]
+    pays = [go(remote(own_pay, own_pay, pay_send.at[m], pay_recv.at[m], mate(m))) for m in range(1, replicas)]
+    own = piece(group, rep)
+    outs = [go(remote(own, own, z_send.at[d], z_recv.at[d], along(d))) for d in range(1, groups)]
+    share(gathered.at[own_rows, :], 0, 0)
 
     positions = lax.broadcasted_iota(jnp.int32, (rows, width), 0)
     hit = positions == picks_ref[0, 0]
     for j in range(1, topk):
         hit = jnp.logical_or(hit, positions == picks_ref[0, j])
     error_out[...] = jnp.where(hit, 0.0, DECAY_RATE * error[...] + grad[...])
-    loads[2].wait()
-    loads[3].wait()
-
-    lanes = lax.broadcasted_iota(jnp.int32, (topk, rows), 1).astype(jnp.float32)
-    for pay in pays:
-        pay.wait_recv()
-    spread = jnp.concatenate(
-        [(payload[m, topk : 2 * topk, 0:1] == lanes).astype(jnp.float32) for m in range(replicas)], axis=0
-    )
-    values = jnp.concatenate([payload[m, :topk, :] for m in range(replicas)], axis=0)
-    summed = lax.dot_general(
-        spread, values, (((0,), (0,)), ((), ())),
-        precision=lax.Precision.HIGHEST, preferred_element_type=jnp.float32,
-    )
-    delta = summed / replicas
-    new_momentum = MOMENTUM_COEF * momentum[...] + delta
-    new_params = params[...] - STEP_SCALE * (delta + MOMENTUM_COEF * new_momentum)
-    own_rows = pl.ds(pl.multiple_of(fsdp * rows, rows), rows)
-    gathered[own_rows, :] = new_params.astype(jnp.bfloat16)
-
-    def piece(g, c, s):
-        return gathered.at[pl.ds(pl.multiple_of((g * 2 + c) * rows + s * part, part), part), :]
-
-    sends = []
-
-    def go(copy):
-        copy.start()
-        sends.append(copy)
-        return copy
-
-    outs = []
-    for d in range(1, groups):
-        own = piece(group, core, rep)
-        outs.append(go(remote(own, own, z_send.at[d], z_recv.at[d], along(d))))
-    whole = gathered.at[own_rows, :]
-    siblings = [go(remote(whole, whole, core_send.at[0, 0], core_recv.at[0, 0], sibling))]
-    params_out[...] = new_params
-    momentum_out[...] = new_momentum
-
-    planes = {}
-    for d in range(1, groups):
+
+    def z_stage(d):
         outs[d - 1].wait_recv()
-        source = lax.rem(group + groups - d, groups)
-        got = piece(source, core, rep)
+        got = piece(source(d), rep)
         for m in range(1, replicas):
             planes[d, m] = go(remote(got, got, plane_send.at[d, m], plane_recv.at[d, m], mate(m)))
-        siblings.append(go(remote(got, got, core_send.at[d, 0], core_recv.at[d, 0], sibling)))
+        share(got, d, 0)
+
+    places = (positions + 1).astype(f32)
+
+    def spread_of(named):
+        return (places == named).astype(f32)[:, :named_rows].astype(bf16)
+
+    def own_stage():
+        for pay in pays:
+            pay.wait_recv()
+        named = sum(payload[m, topk : topk + 1, :] for m in range(replicas))
+        spread = spread_of(named)
+        rest = jnp.concatenate([payload[m, :topk, :] for m in range(replicas)], axis=0)
+        summed = 0.0
+        for _ in range(3):
+            top = rest.astype(bf16)
+            summed = summed + jnp.dot(spread, top, preferred_element_type=f32)
+            rest = rest - top.astype(f32)
+        new_momentum, new_params = step(momentum[...], params[...], summed / replicas)
+        rounded = new_params.astype(bf16)
+        picked = lax.dot_general(spread, rounded, (((0,), (0,)), ((), ())), preferred_element_type=f32)
+        fixes[fsdp, :named_rows, :] = picked.astype(bf16)
+        high = jnp.floor(named / 16)
+        row = lax.broadcasted_iota(jnp.int32, (16, width), 0)
+        digits = jnp.where(row == 0, high, jnp.where(row == 1, named - 16 * high, 0.0))
+        fixes[fsdp, named_rows:, :] = digits.astype(bf16)
+        fix = fixes.at[fsdp]
+        for d in range(1, groups):
+            fix_outs.append(go(remote(fix, fix, fix_send.at[d], fix_recv.at[d], along(d))))
+        fix_siblings.append(go(remote(fix, fix, fix_core_send.at[0], fix_core_recv.at[0], sibling)))
+        params_out[...] = new_params
+        momentum_out[...] = new_momentum
+        final[own_rows, :] = rounded
+
+    def fix_shard(shard):
+        here = pl.ds(pl.multiple_of(shard * rows, rows), rows)
+        digits = fixes[shard, named_rows:, :].astype(f32)
+        spread = spread_of(16 * digits[0:1, :] + digits[1:2, :])
+        total = jnp.dot(spread, fixes[shard, :named_rows, :], preferred_element_type=f32)
+        count = jnp.dot(spread, jnp.ones((named_rows, width), bf16), preferred_element_type=f32)
+        value = total / jnp.maximum(count, 1.0)
+        final[here, :] = jnp.where(count > 0.5, value, gathered[here, :].astype(f32)).astype(bf16)
+
+    fix_outs, fix_siblings = [], []
+    z_stage(1)
+    own_stage()
+    for d in range(2, groups):
+        z_stage(d)
     for d in range(1, groups):
-        source = lax.rem(group + groups - d, groups)
+        fix_outs[d - 1].wait_recv()
+        fix = fixes.at[source(d) * 2 + core]
+        fix_siblings.append(go(remote(fix, fix, fix_core_send.at[d], fix_core_recv.at[d], sibling)))
         for m in range(1, replicas):
             planes[d, m].wait_recv()
-            got = piece(source, core, lax.rem(rep + replicas - m, replicas))
-            siblings.append(go(remote(got, got, core_send.at[d, m], core_recv.at[d, m], sibling)))
-    for copy in siblings:
-        copy.wait_recv()
-    for pay in pays:
-        pay.wait_send()
+            share(piece(source(d), lax.rem(rep + replicas - m, replicas)), d, m)
+    for d in range(1, groups):
+        fix_shard(source(d) * 2 + core)
+    for d in range(groups):
+        fix_siblings[d].wait_recv()
+        for m in range(replicas if d else 1):
+            siblings[d, m].wait_recv()
+        fix_shard(source(d) * 2 + 1 - core)
     for copy in sends:
         copy.wait_send()
 
@@ -169,6 +210,8 @@
             pltpu.VMEM(shard, f32),
             pltpu.VMEM(shard, f32),
             pltpu.VMEM((replicas, 2 * topk, width), f32),
+            pltpu.VMEM((shards * rows, width), bf16),
+            pltpu.VMEM((shards, replicas * topk + 16, width), bf16),
             dma((5,)),
             dma((replicas,)),
             dma((replicas,)),
@@ -178,6 +221,10 @@
             dma((groups, replicas)),
             dma((groups, replicas)),
             dma((groups, replicas)),
+            dma((groups,)),
+            dma((groups,)),
+            dma((groups,)),
+            dma((groups,)),
         ],
         compiler_params=pltpu.CompilerParams(
             collective_id=0, has_side_effects=True, vmem_limit_bytes=32 * 1024 * 1024
@@ -195,8 +242,9 @@
         in_specs=[vmem] * 4,
         out_specs=[hbm] * 4,
         scratch_shapes=[dma((4,))],
+        compiler_params=pltpu.CompilerParams(vmem_limit_bytes=16 * 1024 * 1024),
         name="write_out",
-    )(*held)
+    )(*(pltpu.with_memory_space_constraint(x, pltpu.VMEM) for x in held))
 
 
 def solution(mesh):

time: 32.2 us -> 24.6 us (0.76)
  Pallas kernels: 27.7 us -> 23.8 us
  local copies, waits for them, and re-layouts: 3.7 us -> 0 us
    unnamed x8 -> x0, local copies, waits for them, and re-layouts: 3.7 us -> none
    pallas_call x1, Pallas kernels: 3.94 us -> 1.86 us  [per_device(): pl.pallas_call(write_kernel, out_shape=(jax.ShapeDtypeStruct(shard, f32),...]
    pallas_call x1, Pallas kernels: 23.7 us -> 21.9 us  [per_device(): pl.pallas_call(functools.partial(exchange_kernel, replicas, shards, topk)...]
where the time goes in v3:
time: 24.6 us; the launch traced here: 24.4 us
  Pallas kernels  23.8 us (97%)
  between operations  0.64 us (3%)
    pallas_call x1, Pallas kernels, per_device(): pl.pallas_call(functools.partial(exchange_kernel, replicas, shards, topk)...  21.9 us
    pallas_call x1, Pallas kernels, per_device(): pl.pallas_call(write_kernel, out_shape=(jax.ShapeDtypeStruct(shard, f32),...  1.86 us

profile of v3, /device:TPU:0, one launch (start us, length us, event | category | flops | bytes accessed | tf_op | source)
XLA Modules:
  0.0 24.4 jit_solution(3436265896750626636)
XLA Ops:
  0.6 21.9 %exchange.1 = (f32[512,256]{1,0:T(8,128)S(1)}, f32[512,256]{1,0:T(8,128)S(1)}, f32[512,256]{1,0:T(8,128)S(1)}, bf16[4096,256]{1,0:T(8,128)(2,1)S(1)}) custom-call(s32[1,8]{1,0:T(1,128)} %picks_hbm.1, f32[1,512,256]{2,1,0:T(8,128)} %grad_hbm.1, f32[1,512,256]{2,1,0:T(8,128)} %error_hbm.1, f32[512,256]{1,0:T(8,128)} %momentum_hbm.1, f32[512,256]{1,0:T(8,128)} %params_hbm.1), custom_call_target="tpu_custom_call" | custom-call | tf_op jit(solution)/shard_map/exchange/pallas_call | solution.py:196
  22.5 1.9 %write_out.1 = (f32[512,256]{1,0:T(8,128)}, f32[512,256]{1,0:T(8,128)}, f32[1,512,256]{2,1,0:T(8,128)}, bf16[4096,256]{1,0:T(8,128)(2,1)}) custom-call(f32[512,256]{1,0:T(8,128)S(1)} %get-tuple-element.8.params, f32[512,256]{1,0:T(8,128)S(1)} %get-tuple-element.9.momentum, f32[512,256]{1,0:T(8,128)S(1)} %get-tuple-element.10.error, ...), custom_call_target="tpu_custom_call" | custom-call | tf_op jit(solution)/shard_map/write_out/pallas_call | solution.py:234

commit v4 on v3

--- a/solution.py
+++ b/solution.py
@@ -65,6 +65,52 @@
     own_rows = pl.ds(pl.multiple_of(fsdp * rows, rows), rows)
     gathered[own_rows, :] = step(momentum[...], params[...], 0.0)[1].astype(bf16)
 
+    def piece(g, s):
+        return gathered.at[pl.ds(pl.multiple_of((g * 2 + core) * rows + s * part, part), part), :]
+
+    def source(d):
+        return lax.rem(group + groups - d, groups)
+
+    sends = []
+
+    def go(copy):
+        copy.start()
+        sends.append(copy)
+        return copy
+
+    def on_line(g):
+        return jnp.logical_and(g >= 0, g < groups)
+
+    def came_from(w, j):
+        return group + (j if w else -j)
+
+    def onward(w):
+        return group + (-1 if w else 1)
+
+    def hop(w, j):
+        ref = piece(came_from(w, j), rep)
+        to = (rep, onward(w) * 2 + core)
+        return remote(ref, ref, z_send.at[w, j], z_recv.at[w, j], to)
+
+    def arrives(w, j):
+        return on_line(came_from(w, j))
+
+    def goes(w, j):
+        return jnp.logical_and(arrives(w, j), on_line(onward(w)))
+
+    def plane(w, j, m):
+        ref = piece(came_from(w, j), rep)
+        return remote(ref, ref, plane_send.at[w, j, m], plane_recv.at[w, j, m], mate(m))
+
+    def pair(w, j, m):
+        ref = piece(came_from(w, j), lax.rem(rep + replicas - m, replicas))
+        return remote(ref, ref, core_send.at[w, j, m], core_recv.at[w, j, m], sibling)
+
+    hops = [(w, j) for j in range(1, groups) for w in range(2)]
+    pl.semaphore_wait(barrier, len(partners))
+    for w in range(2):
+        pl.when(on_line(onward(w)))(hop(w, 0).start)
+
     loads[3].wait()
     loads[4].wait()
     lane = lax.broadcasted_iota(jnp.int32, (1, width), 1)
@@ -74,29 +120,11 @@
         payload[rep, j, :] = DECAY_RATE * error[pick, :] + grad[pick, :]
         numbers = jnp.where(lane == rep * topk + j, (pick + 1).astype(f32), numbers)
     payload[rep, topk : 2 * topk, :] = jnp.broadcast_to(numbers, (topk, width))
-    pl.semaphore_wait(barrier, len(partners))
-
-    def piece(g, s):
-        return gathered.at[pl.ds(pl.multiple_of((g * 2 + core) * rows + s * part, part), part), :]
-
-    def source(d):
-        return lax.rem(group + groups - d, groups)
-
-    sends, siblings, planes = [], {}, {}
-
-    def go(copy):
-        copy.start()
-        sends.append(copy)
-        return copy
-
-    def share(ref, d, m):
-        siblings[d, m] = go(remote(ref, ref, core_send.at[d, m], core_recv.at[d, m], sibling))
 
     own_pay = payload.at[rep]
     pays = [go(remote(own_pay, own_pay, pay_send.at[m], pay_recv.at[m], mate(m))) for m in range(1, replicas)]
-    own = piece(group, rep)
-    outs = [go(remote(own, own, z_send.at[d], z_recv.at[d], along(d))) for d in range(1, groups)]
-    share(gathered.at[own_rows, :], 0, 0)
+    own_whole = gathered.at[own_rows, :]
+    whole = go(remote(own_whole, own_whole, core_send.at[0, 0, 0], core_recv.at[0, 0, 0], sibling))
 
     positions = lax.broadcasted_iota(jnp.int32, (rows, width), 0)
     hit = positions == picks_ref[0, 0]
@@ -104,12 +132,37 @@
         hit = jnp.logical_or(hit, positions == picks_ref[0, j])
     error_out[...] = jnp.where(hit, 0.0, DECAY_RATE * error[...] + grad[...])
 
-    def z_stage(d):
-        outs[d - 1].wait_recv()
-        got = piece(source(d), rep)
-        for m in range(1, replicas):
-            planes[d, m] = go(remote(got, got, plane_send.at[d, m], plane_recv.at[d, m], mate(m)))
-        share(got, d, 0)
+    def z_stage(w, j):
+        @pl.when(arrives(w, j))
+        def _():
+            hop(w, j - 1).wait_recv()
+            if j + 1 < groups:
+                pl.when(on_line(onward(w)))(hop(w, j).start)
+            for m in range(1, replicas):
+                plane(w, j, m).start()
+            pair(w, j, 0).start()
+
+    def plane_stage(w, j):
+        @pl.when(arrives(w, j))
+        def _():
+            for m in range(1, replicas):
+                plane(w, j, m).wait_recv()
+                pair(w, j, m).start()
+
+    def last_stage(w, j):
+        @pl.when(arrives(w, j))
+        def _():
+            for m in range(replicas):
+                pair(w, j, m).wait_recv()
+            fix_shard(came_from(w, j) * 2 + 1 - core)
+
+    def drain(w, j):
+        @pl.when(arrives(w, j))
+        def _():
+            for m in range(replicas):
+                pair(w, j, m).wait_send()
+                if m:
+                    plane(w, j, m).wait_send()
 
     places = (positions + 1).astype(f32)
 
@@ -148,29 +201,36 @@
         digits = fixes[shard, named_rows:, :].astype(f32)
         spread = spread_of(16 * digits[0:1, :] + digits[1:2, :])
         total = jnp.dot(spread, fixes[shard, :named_rows, :], preferred_element_type=f32)
-        count = jnp.dot(spread, jnp.ones((named_rows, width), bf16), preferred_element_type=f32)
+        count = jnp.dot(spread, jnp.ones((named_rows, width // 2), bf16), preferred_element_type=f32)
+        count = jnp.concatenate([count, count], axis=1)
         value = total / jnp.maximum(count, 1.0)
         final[here, :] = jnp.where(count > 0.5, value, gathered[here, :].astype(f32)).astype(bf16)
 
     fix_outs, fix_siblings = [], []
-    z_stage(1)
+    for w in range(2):
+        z_stage(w, 1)
     own_stage()
-    for d in range(2, groups):
-        z_stage(d)
+    for w, j in hops[2:]:
+        z_stage(w, j)
     for d in range(1, groups):
         fix_outs[d - 1].wait_recv()
         fix = fixes.at[source(d) * 2 + core]
         fix_siblings.append(go(remote(fix, fix, fix_core_send.at[d], fix_core_recv.at[d], sibling)))
-        for m in range(1, replicas):
-            planes[d, m].wait_recv()
-            share(piece(source(d), lax.rem(rep + replicas - m, replicas)), d, m)
+    for w, j in hops:
+        plane_stage(w, j)
     for d in range(1, groups):
         fix_shard(source(d) * 2 + core)
-    for d in range(groups):
-        fix_siblings[d].wait_recv()
-        for m in range(replicas if d else 1):
-            siblings[d, m].wait_recv()
-        fix_shard(source(d) * 2 + 1 - core)
+    for fix in fix_siblings:
+        fix.wait_recv()
+    whole.wait_recv()
+    fix_shard(group * 2 + 1 - core)
+    for w, j in hops:
+        last_stage(w, j)
+    for w in range(2):
+        for j in range(groups - 1):
+            pl.when(goes(w, j))(hop(w, j).wait_send)
+    for w, j in hops:
+        drain(w, j)
     for copy in sends:
         copy.wait_send()
 
@@ -215,12 +275,12 @@
             dma((5,)),
             dma((replicas,)),
             dma((replicas,)),
-            dma((groups,)),
-            dma((groups,)),
-            dma((groups, replicas)),
-            dma((groups, replicas)),
-            dma((groups, replicas)),
-            dma((groups, replicas)),
+            dma((2, groups)),
+            dma((2, groups)),
+            dma((2, groups, replicas)),
+            dma((2, groups, replicas)),
+            dma((2, groups, replicas)),
+            dma((2, groups, replicas)),
             dma((groups,)),
             dma((groups,)),
             dma((groups,)),

time: 24.6 us -> 25.9 us (1.053)
  Pallas kernels: 23.8 us -> 25.1 us
    pallas_call x1, Pallas kernels: 21.9 us -> 23.2 us  [per_device(): pl.pallas_call(functools.partial(exchange_kernel, replicas, shards, topk)...]
where the time goes in v4:
time: 25.9 us; the launch traced here: 25.7 us
  Pallas kernels  25.1 us (97%)
  between operations  0.64 us (2%)
    pallas_call x1, Pallas kernels, per_device(): pl.pallas_call(functools.partial(exchange_kernel, replicas, shards, topk)...  23.2 us
    pallas_call x1, Pallas kernels, per_device(): pl.pallas_call(write_kernel, out_shape=(jax.ShapeDtypeStruct(shard, f32),...  1.86 us

profile of v4, /device:TPU:0, one launch (start us, length us, event | category | flops | bytes accessed | tf_op | source)
XLA Modules:
  0.0 25.7 jit_solution(13583985243062795837)
XLA Ops:
  0.6 23.2 %exchange.1 = (f32[512,256]{1,0:T(8,128)S(1)}, f32[512,256]{1,0:T(8,128)S(1)}, f32[512,256]{1,0:T(8,128)S(1)}, bf16[4096,256]{1,0:T(8,128)(2,1)S(1)}) custom-call(s32[1,8]{1,0:T(1,128)} %picks_hbm.1, f32[1,512,256]{2,1,0:T(8,128)} %grad_hbm.1, f32[1,512,256]{2,1,0:T(8,128)} %error_hbm.1, f32[512,256]{1,0:T(8,128)} %momentum_hbm.1, f32[512,256]{1,0:T(8,128)} %params_hbm.1), custom_call_target="tpu_custom_call" | custom-call | tf_op jit(solution)/shard_map/exchange/pallas_call | solution.py:256
  23.9 1.9 %write_out.1 = (f32[512,256]{1,0:T(8,128)}, f32[512,256]{1,0:T(8,128)}, f32[1,512,256]{2,1,0:T(8,128)}, bf16[4096,256]{1,0:T(8,128)(2,1)}) custom-call(f32[512,256]{1,0:T(8,128)S(1)} %get-tuple-element.8.params, f32[512,256]{1,0:T(8,128)S(1)} %get-tuple-element.9.momentum, f32[512,256]{1,0:T(8,128)S(1)} %get-tuple-element.10.error, ...), custom_call_target="tpu_custom_call" | custom-call | tf_op jit(solution)/shard_map/write_out/pallas_call | solution.py:294
